TPU v7x, 32 devices: a whole 2x2x4 slice. The times are simulated.
32 devices in a mesh: chan: 8 (over z, core), tm: 4 (over y, x).
Axes of the slice: x: 2, y: 2, z: 4, core: 2. Of those that a mesh axis runs over, the one named last changes fastest.
Arguments:
- samples: bfloat16 [512, 32, 512], P('chan', 'tm'), may hold values from -6 to 6
- valid: int32 [512, 32], P('chan', 'tm'), may hold values 0 or 1
- offsets: int32 [8], replicated, may hold values from 0 to 31
Outputs:
- correlations: bfloat16 [4, 8, 512, 512], P('tm', None, 'chan')
All inputs are finite; a program needn't handle non-finite values. No bound on the sum of `valid` on one device may be relied on, other than what follows from the above.
Results may differ from a plain program's by a relative error of at most 0.0045.
Values may be sent and summed in bfloat16 or wider, within the bound.
No kernel may reach another device: no remote copies, remote signals or barrier semaphores. Data moves between devices by JAX's collectives and lax.ppermute only.
A program may use at most 64 MiB of HBM per device.

v0:
```python
import functools
import math

import jax
import jax.numpy as jnp
import numpy as np
from jax import lax
from jax.experimental import pallas as pl
from jax.experimental.pallas import tpu as pltpu
from jax.sharding import PartitionSpec as P

OFFSET_SPAN = 32
LANES = 128
DECAY = 0.99
VMEM = 24 * 1024 * 1024


def turns(number, length):
    part = (number - length * jnp.floor(number / length + 0.5)) * (1.0 / length)
    square = part * part
    cosine, sine = jnp.float32(0.0), jnp.float32(0.0)
    for k in range(10, -1, -1):
        cosine = cosine * square + (-1) ** k * (2 * math.pi) ** (2 * k) / math.factorial(2 * k)
        sine = sine * square + (-1) ** k * (2 * math.pi) ** (2 * k + 1) / math.factorial(2 * k + 1)
    return cosine, sine * part


def fill_table(table_ref, step):
    length = table_ref.shape[0]
    bins = length // 2

    def small(rows, by):
        row = lax.broadcasted_iota(jnp.int32, (rows, bins), 0)
        freq = lax.broadcasted_iota(jnp.int32, (rows, bins), 1) + 1
        return turns((row * (by * freq)).astype(jnp.float32), length)

    coarse_cos, coarse_sin = small(length // step, step)
    fine_cos, fine_sin = small(step, 1)
    for i in range(length // step):
        rows = slice(i * step, (i + 1) * step)
        cos_i, sin_i = coarse_cos[i : i + 1], coarse_sin[i : i + 1]
        table_ref[rows, :bins] = (cos_i * fine_cos - sin_i * fine_sin).astype(jnp.bfloat16)
        table_ref[rows, bins:] = -(sin_i * fine_cos + cos_i * fine_sin).astype(jnp.bfloat16)


def whiten_block(x, table, keep, raw_ref, white_ref, short_ref):
    wins, span, length = white_ref.shape
    bins = length // 2
    tiles = bins // LANES
    raw = jnp.dot(x, table, preferred_element_type=jnp.float32)
    for t in range(2 * tiles):
        raw_ref[t] = raw[:, t * LANES : (t + 1) * LANES]
    for w in range(wins):
        part = [raw_ref[t, pl.ds(w, span, stride=wins), :] for t in range(2 * tiles)]
        power = [part[t] * part[t] + part[tiles + t] * part[tiles + t] for t in range(tiles)]
        total = power[0]
        for t in range(1, tiles):
            total = total + power[t]
        level = jnp.sum(total, axis=-1, keepdims=True) * (0.01 / bins) + 1e-06
        alive = keep[:, w * LANES : (w + 1) * LANES]
        for t in range(tiles):
            scale = alive * lax.rsqrt(power[t] + level)
            for s in (t, tiles + t):
                value = part[s] * scale
                here = pl.ds(w * length + s * LANES, LANES)
                white_ref[w, :, s * LANES : (s + 1) * LANES] = value
                short_ref[:, here] = value.astype(jnp.bfloat16)


def head_kernel(
    x_hbm,
    valid_hbm,
    offsets_hbm,
    white_ref,
    short_ref,
    table_ref,
    pick_ref,
    keep_ref,
    x_ref,
    valid_ref,
    offsets_ref,
    raw_ref,
    sems,
):
    wins, span, length = white_ref.shape
    pairs = offsets_ref.shape[0]
    copies = [
        pltpu.make_async_copy(valid_hbm, valid_ref, sems.at[0]),
        pltpu.make_async_copy(offsets_hbm, offsets_ref, sems.at[1]),
        pltpu.make_async_copy(x_hbm.at[pl.ds(0, span * wins)], x_ref, sems.at[2]),
    ]
    for copy in copies:
        copy.start()
    fill_table(table_ref, 16)
    copies[0].wait()
    copies[1].wait()
    ahead = lax.broadcasted_iota(jnp.int32, (span, 2 * span), 1) - lax.broadcasted_iota(
        jnp.int32, (span, 2 * span), 0
    )
    for k in range(pairs):
        chosen_row = jnp.where(ahead == offsets_ref[k], jnp.float32(1.0), jnp.float32(0.0))
        pick_ref[k] = chosen_row.astype(jnp.bfloat16)
    owner = lax.broadcasted_iota(jnp.int32, (wins, wins * LANES), 0)
    column = lax.broadcasted_iota(jnp.int32, (wins, wins * LANES), 1) // LANES
    keep_ref[...] = lax.dot_general(
        valid_ref[...].astype(jnp.float32).astype(jnp.bfloat16),
        (owner == column).astype(jnp.float32).astype(jnp.bfloat16),
        (((0,), (0,)), ((), ())),
        preferred_element_type=jnp.float32,
    )
    copies[2].wait()
    whiten_block(x_ref[...], table_ref[...], keep_ref[:span], raw_ref, white_ref, short_ref)


def stack_pairs(pick_ref, white_ref, near_ref, parts_ref, out_ref):
    wins, _, length = white_ref.shape
    pairs, rows, reach = pick_ref.shape
    bins = length // 2
    pick = pick_ref[...].reshape(pairs * rows, reach)
    decay = [float(np.float32(DECAY) ** np.float32(wins - 1 - w)) for w in range(wins)]
    for w in range(wins):
        parts_ref[w] = jnp.dot(
            pick, near_ref[:, w * length : (w + 1) * length], preferred_element_type=jnp.float32
        )
    for c in range(0, rows, 16):
        for t in range(bins // LANES):
            re = slice(t * LANES, (t + 1) * LANES)
            im = slice(bins + t * LANES, bins + (t + 1) * LANES)
            head_re = [white_ref[w, c : c + 16, re] * decay[w] for w in range(wins)]
            head_im = [white_ref[w, c : c + 16, im] * decay[w] for w in range(wins)]
            for k in range(pairs):
                here = slice(k * rows + c, k * rows + c + 16)
                total_re = total_im = None
                for w in range(wins):
                    part_re, part_im = parts_ref[w, here, re], parts_ref[w, here, im]
                    cross_re = head_re[w] * part_re + head_im[w] * part_im
                    cross_im = head_im[w] * part_re - head_re[w] * part_im
                    total_re = cross_re if w == 0 else total_re + cross_re
                    total_im = cross_im if w == 0 else total_im + cross_im
                out_ref[k, c : c + 16, re] = total_re.astype(out_ref.dtype)
                out_ref[k, c : c + 16, im] = total_im.astype(out_ref.dtype)


def tail_kernel(
    x_ref, table_ref, keep_ref, pick_ref, head_ref, edge_ref, white_ref, short_ref, out_ref, raw_ref, near_ref, parts_ref
):
    wins, span, length = white_ref.shape
    rows = slice(span * wins, 2 * span * wins)
    whiten_block(x_ref[rows, :], table_ref[...], keep_ref[span:], raw_ref, white_ref, short_ref)
    near_ref[:span] = edge_ref[...]
    near_ref[span:] = short_ref[...]
    stack_pairs(pick_ref, head_ref, near_ref, parts_ref, out_ref)


def cross_kernel(pick_ref, white_ref, short_ref, edge_ref, out_ref, near_ref, parts_ref):
    span = short_ref.shape[0]
    near_ref[:span] = short_ref[...]
    near_ref[span:] = edge_ref[...]
    stack_pairs(pick_ref, white_ref, near_ref, parts_ref, out_ref)


def chosen(options, place):
    value = jnp.float32(options[0])
    for i, option in enumerate(options[1:]):
        value = jnp.where(place == i + 1, jnp.float32(option), value)
    return value


def weighted(terms, weights, place):
    total = None
    for term, options in zip(terms, weights):
        value = term[...].astype(jnp.float32)
        if set(options) != {1.0}:
            value = value * (options[0] if len(set(options)) == 1 else chosen(options, place))
        total = value if total is None else total + value
    return total


def mix_kernel(weights, *refs):
    place = lax.axis_index("tm")
    total = weighted(refs[: len(weights)], weights, place)
    refs[-1][...] = total.astype(refs[-1].dtype)


def lag_kernel(scale, first, weights, table_ref, *rest):
    out_hbm, stage_ref, sems = rest[-3:]
    place = lax.axis_index("tm")
    dims = (((1,), (1,)), ((), ()))
    pairs, rows, length = stage_ref.shape
    refs = rest[: len(weights)]
    stack = weighted(refs, weights, place).reshape(pairs * rows, length)
    high = stack.astype(jnp.bfloat16)
    low = (stack - high.astype(jnp.float32)).astype(jnp.bfloat16)
    table = table_ref[...]
    lagged = lax.dot_general(high, table, dims, preferred_element_type=jnp.float32)
    lagged = lagged + lax.dot_general(low, table, dims, preferred_element_type=jnp.float32)
    stage_ref[...] = (lagged * scale).astype(stage_ref.dtype).reshape(pairs, rows, length)
    copy = pltpu.make_async_copy(stage_ref, out_hbm.at[:, pl.ds(first, rows)], sems.at[0])
    copy.start()
    copy.wait()


def cost(flops, moved):
    return pl.CostEstimate(flops=flops, bytes_accessed=moved, transcendentals=0)


def whole(memory=pltpu.VMEM):
    return pl.BlockSpec(memory_space=memory)


def per_device(samples, valid, offsets):
    chans, wins, length = samples.shape
    bins = length // 2
    span = OFFSET_SPAN
    pairs = offsets.shape[0]
    tiles = bins // LANES
    groups = lax.axis_size("tm")
    factor = float(np.float32(DECAY) ** np.float32(wins))
    params = pltpu.CompilerParams(vmem_limit_bytes=VMEM)

    def in_hbm(value):
        return pltpu.with_memory_space_constraint(value, pltpu.HBM)

    half = chans - span
    flat = samples.reshape(chans * wins, length)
    white_type = jax.ShapeDtypeStruct((wins, span, length), jnp.float32)
    short_type = jax.ShapeDtypeStruct((span, wins * length), jnp.bfloat16)
    local_type = jax.ShapeDtypeStruct((pairs, span, length), jnp.bfloat16)
    raw_scratch = pltpu.VMEM((2 * tiles, span * wins, LANES), jnp.float32)
    near_scratch = pltpu.VMEM((2 * span, wins * length), jnp.bfloat16)
    parts_scratch = pltpu.VMEM((wins, pairs * span, length), jnp.float32)

    white_a, short_a, table, pick, keep = pl.pallas_call(
        head_kernel,
        out_shape=(
            white_type,
            short_type,
            jax.ShapeDtypeStruct((length, length), jnp.bfloat16),
            jax.ShapeDtypeStruct((pairs, span, 2 * span), jnp.bfloat16),
            jax.ShapeDtypeStruct((chans, wins * LANES), jnp.float32),
        ),
        in_specs=[whole(pltpu.HBM)] * 3,
        out_specs=(whole(),) * 5,
        scratch_shapes=[
            pltpu.VMEM((span * wins, length), jnp.bfloat16),
            pltpu.VMEM((wins, chans), jnp.int32),
            pltpu.SMEM((pairs,), jnp.int32),
            raw_scratch,
            pltpu.SemaphoreType.DMA((3,)),
        ],
        compiler_params=params,
        cost_estimate=cost(span * wins * length * length * 2, 2 * 1024 * 1024),
        name="head",
    )(in_hbm(flat), in_hbm(valid.T), in_hbm(offsets))

    ring = lax.axis_size("chan")
    edge = lax.ppermute(short_a, "chan", [(i, i - 1) for i in range(1, ring)])

    white_b, short_b, local_a = pl.pallas_call(
        tail_kernel,
        out_shape=(white_type, short_type, local_type),
        in_specs=[whole()] * 6,
        out_specs=(whole(),) * 3,
        scratch_shapes=[raw_scratch, near_scratch, parts_scratch],
        compiler_params=params,
        cost_estimate=cost(span * wins * length * length * 4, 4 * 1024 * 1024),
        name="tail",
    )(flat, table, keep, pick, white_a, short_a)

    local_b = pl.pallas_call(
        cross_kernel,
        out_shape=local_type,
        in_specs=[whole()] * 4,
        out_specs=whole(),
        scratch_shapes=[near_scratch, parts_scratch],
        compiler_params=params,
        cost_estimate=cost(pairs * span * wins * bins * 8, 4 * 1024 * 1024),
        name="cross",
    )(pick, white_b, short_b, edge)

    power = [float(np.float32(factor) ** np.float32(d)) for d in range(groups)]
    columns = min(d for d in range(1, groups + 1) if groups % d == 0 and d * d >= groups)
    square = columns == 2 and groups == columns * columns

    def sent(value, moves):
        return lax.ppermute(value, "tm", moves)

    def faded(moves):
        origin = {there: here for here, there in moves}
        return [power[h - origin[h]] if h in origin else 0.0 for h in range(groups)]

    if square:
        low, high = [(0, 1), (1, 3)], [(0, 2), (2, 3)]
        straight = [[(0, 3), (1, 2)], low, high]
    else:
        straight = [[(h, h + d) for h in range(groups - d)] for d in range(1, groups)]

    def mix(terms, weights, after):
        return pl.pallas_call(
            functools.partial(mix_kernel, weights),
            out_shape=local_type,
            in_specs=[whole()] * len(terms) + [whole(pl.ANY)],
            out_specs=whole(),
            compiler_params=params,
            cost_estimate=cost(len(terms) * terms[0].size * 4, 1024 * 1024),
            name="mix",
        )(*terms, after)

    def lags(first, terms, weights, *so_far):
        return pl.pallas_call(
            functools.partial(lag_kernel, bins**-0.5, first, weights),
            out_shape=jax.ShapeDtypeStruct((pairs, chans, length), jnp.bfloat16),
            in_specs=[whole()] * (1 + len(terms)) + [whole(pl.ANY)] * len(so_far),
            out_specs=whole(pl.ANY),
            scratch_shapes=[
                pltpu.VMEM((pairs, span, length), jnp.bfloat16),
                pltpu.SemaphoreType.DMA((1,)),
            ],
            input_output_aliases={1 + len(terms): 0} if so_far else {},
            compiler_params=params,
            cost_estimate=cost(pairs * span * length * length * 4, 1024 * 1024),
            name="lags",
        )(table, *terms, *so_far)

    unit = [1.0] * groups
    terms_b = [local_b] + [sent(local_b, moves) for moves in straight]
    weights_b = [unit] + [faded(moves) for moves in straight]
    if square:
        got_low, got_high = sent(local_a, low), sent(local_a, high)
        onward = mix([got_low, got_high], [[0.0, 0.0, 0.0, 1.0], [0.0, 0.0, 1.0, 0.0]], local_b)
        terms_a = [local_a, got_low, got_high, sent(onward, [(2, 3), (3, 2)])]
        weights_a = [unit, faded(low), faded(high), [0.0, 0.0, power[1], power[3]]]
    else:
        terms_a = [local_a] + [sent(local_a, moves) for moves in straight]
        weights_a = weights_b
    result = lags(half, terms_b, weights_b)
    result = lags(0, terms_a, weights_a, result)
    return result.reshape(1, pairs, chans, length)


def solution(mesh):
    in_specs = (P("chan", "tm", None), P("chan", "tm"), P())
    out_specs = P("tm", None, "chan", None)
    return jax.shard_map(
        per_device, mesh=mesh, in_specs=in_specs, out_specs=out_specs, check_vma=False
    )
```

profile of v0, /device:TPU:28, one launch (start us, length us, event | category | flops | bytes accessed | tf_op | source)
XLA Modules:
  0.0 33.6 jit_solution(17292564476634098255)
XLA Ops:
  0.0 0.0 copy-start
  0.0 1.5 %head.1 = (f32[8,32,512]{2,1,0:T(8,128)S(1)}, bf16[32,4096]{1,0:T(8,128)(2,1)S(1)}, bf16[512,512]{1,0:T(8,128)(2,1)S(1)}, bf16[8,32,64]{2,1,0:T(8,128)(2,1)S(1)}, f32[64,1024]{1,0:T(8,128)S(1)}) custom-call(bf16[512,512]{1,0:T(8,128)(2,1)} %bitcast.3, s32[8,64]{1,0:T(8,128)} %bitcast.5, s32[8]{0:T(128)} %offsets_hbm.1), custom_call_target="tpu_custom_call" | custom-call | flops 134217728 | bytes 2097152 | tf_op jit(solution)/shard_map/head/pallas_call | solution.py:233
  1.5 1.9 %collective-permute-start.2 = (bf16[32,4096]{1,0:T(8,128)(2,1)S(1)}, bf16[32,4096]{1,0:T(8,128)(2,1)S(1)}, u32[]{:S(2)}, u32[]{:S(2)}) collective-permute-start(bf16[32,4096]{1,0:T(8,128)(2,1)S(1)} %get-tuple-element.17.edge_ref), channel_id=1, source_target_pairs={{4,0},{8,4},{12,8},{16,12},{20,16},{24,20},{28,24},{5,1},{9,5},{13... | collective-permute-start | bytes 786440 | tf_op jit(solution)/shard_map/ppermute | solution.py:257
  3.4 0.0 copy-done
  3.5 1.4 %tail.1 = (f32[8,32,512]{2,1,0:T(8,128)S(1)}, bf16[32,4096]{1,0:T(8,128)(2,1)S(1)}, bf16[8,32,512]{2,1,0:T(8,128)(2,1)S(1)}) custom-call(bf16[512,512]{1,0:T(8,128)(2,1)S(1)} %bitcast.4, bf16[512,512]{1,0:T(8,128)(2,1)S(1)} %get-tuple-element.13.table_ref, f32[64,1024]{1,0:T(8,128)S(1)} %get-tuple-element.14.keep_ref, ...), custom_call_target="tpu_custom_call" | custom-call | flops 268435456 | bytes 4194304 | tf_op jit(solution)/shard_map/tail/pallas_call | solution.py:259
  4.9 0.7 %collective-permute-start = (bf16[8,32,512]{2,1,0:T(8,128)(2,1)S(1)}, bf16[8,32,512]{2,1,0:T(8,128)(2,1)S(1)}, u32[]{:S(2)}, u32[]{:S(2)}) collective-permute-start(bf16[8,32,512]{2,1,0:T(8,128)(2,1)S(1)} %get-tuple-element.18.rest_0_), channel_id=1, source_target_pairs={{0,1},{1,3},{4,5},{5,7},{8,9},{9,11},{12,13},{13,15},{16,17},{17,1... | collective-permute-start | bytes 786440 | tf_op jit(solution)/shard_map/ppermute | solution.py:286
  5.6 4.0 %collective-permute-start.1 = (bf16[8,32,512]{2,1,0:T(8,128)(2,1)S(1)}, bf16[8,32,512]{2,1,0:T(8,128)(2,1)S(1)}, u32[]{:S(2)}, u32[]{:S(2)}) collective-permute-start(bf16[8,32,512]{2,1,0:T(8,128)(2,1)S(1)} %get-tuple-element.18.rest_0_), channel_id=1, source_target_pairs={{0,2},{2,3},{4,6},{6,7},{8,10},{10,11},{12,14},{14,15},{16,18},{18... | collective-permute-start | bytes 786440 | tf_op jit(solution)/shard_map/ppermute | solution.py:286
  9.6 0.0 collective-permute-done.2.edge_ref
  9.6 1.0 %cross.1.refs_2_.rest_0_ = bf16[8,32,512]{2,1,0:T(8,128)(2,1)S(1)} custom-call(bf16[8,32,64]{2,1,0:T(8,128)(2,1)S(1)} %get-tuple-element.15.pick_ref, f32[8,32,512]{2,1,0:T(8,128)S(1)} %get-tuple-element.19.white_ref, bf16[32,4096]{1,0:T(8,128)(2,1)S(1)} %get-tuple-element.20.short_ref, bf16[32,4096]{1,0:T(8,128)(2,1)S(1)} %collective-permute-done.2.edge_ref), custom_call_target="tpu_custom_call" | custom-call | flops 4194304 | bytes 4194304 | tf_op jit(solution)/shard_map/cross/pallas_call | solution.py:270
  10.6 1.3 %collective-permute-start.4 = (bf16[8,32,512]{2,1,0:T(8,128)(2,1)S(1)}, bf16[8,32,512]{2,1,0:T(8,128)(2,1)S(1)}, u32[]{:S(2)}, u32[]{:S(2)}) collective-permute-start(bf16[8,32,512]{2,1,0:T(8,128)(2,1)S(1)} %cross.1.refs_2_.rest_0_), channel_id=1, source_target_pairs={{0,3},{1,2},{4,7},{5,6},{8,11},{9,10},{12,15},{13,14},{16,19},{17,... | collective-permute-start | bytes 786440 | tf_op jit(solution)/shard_map/ppermute | solution.py:286
  11.9 0.7 %collective-permute-start.5 = (bf16[8,32,512]{2,1,0:T(8,128)(2,1)S(1)}, bf16[8,32,512]{2,1,0:T(8,128)(2,1)S(1)}, u32[]{:S(2)}, u32[]{:S(2)}) collective-permute-start(bf16[8,32,512]{2,1,0:T(8,128)(2,1)S(1)} %cross.1.refs_2_.rest_0_), channel_id=1, source_target_pairs={{0,1},{1,3},{4,5},{5,7},{8,9},{9,11},{12,13},{13,15},{16,17},{17,1... | collective-permute-start | bytes 786440 | tf_op jit(solution)/shard_map/ppermute | solution.py:286
  12.6 1.9 %collective-permute-start.6 = (bf16[8,32,512]{2,1,0:T(8,128)(2,1)S(1)}, bf16[8,32,512]{2,1,0:T(8,128)(2,1)S(1)}, u32[]{:S(2)}, u32[]{:S(2)}) collective-permute-start(bf16[8,32,512]{2,1,0:T(8,128)(2,1)S(1)} %cross.1.refs_2_.rest_0_), channel_id=1, source_target_pairs={{0,2},{2,3},{4,6},{6,7},{8,10},{10,11},{12,14},{14,15},{16,18},{18... | collective-permute-start | bytes 786440 | tf_op jit(solution)/shard_map/ppermute | solution.py:286
  14.5 0.0 collective-permute-done.refs_0_.rest_1_
  14.5 8.3 %collective-permute-done.1.refs_1_.rest_2_ = bf16[8,32,512]{2,1,0:T(8,128)(2,1)S(1)} collective-permute-done((bf16[8,32,512]{2,1,0:T(8,128)(2,1)S(1)}, bf16[8,32,512]{2,1,0:T(8,128)(2,1)S(1)}, u32[]{:S(2)}, u32[]{:S(2)}) %collective-permute-start.1) | collective-permute-done | bytes 262176 | tf_op jit(solution)/shard_map/ppermute | solution.py:286
  22.8 0.1 mix.1
  22.9 1.9 %collective-permute-start.3 = (bf16[8,32,512]{2,1,0:T(8,128)(2,1)S(1)}, bf16[8,32,512]{2,1,0:T(8,128)(2,1)S(1)}, u32[]{:S(2)}, u32[]{:S(2)}) collective-permute-start(bf16[8,32,512]{2,1,0:T(8,128)(2,1)S(1)} %mix.1), channel_id=1, source_target_pairs={{2,3},{3,2},{6,7},{7,6},{10,11},{11,10},{14,15},{15,14},{18,19},{1... | collective-permute-start | bytes 786440 | tf_op jit(solution)/shard_map/ppermute | solution.py:286
  24.8 0.0 collective-permute-done.4.rest_1_
  24.8 0.0 collective-permute-done.5.rest_2_
  24.9 3.2 %collective-permute-done.6.rest_3_ = bf16[8,32,512]{2,1,0:T(8,128)(2,1)S(1)} collective-permute-done((bf16[8,32,512]{2,1,0:T(8,128)(2,1)S(1)}, bf16[8,32,512]{2,1,0:T(8,128)(2,1)S(1)}, u32[]{:S(2)}, u32[]{:S(2)}) %collective-permute-start.6) | collective-permute-done | bytes 262176 | tf_op jit(solution)/shard_map/ppermute | solution.py:286
  28.0 1.2 %lags.2.rest_4_ = bf16[8,64,512]{2,1,0:T(8,128)(2,1)} custom-call(bf16[512,512]{1,0:T(8,128)(2,1)S(1)} %get-tuple-element.13.table_ref, bf16[8,32,512]{2,1,0:T(8,128)(2,1)S(1)} %cross.1.refs_2_.rest_0_, bf16[8,32,512]{2,1,0:T(8,128)(2,1)S(1)} %collective-permute-done.4.rest_1_, bf16[8,32,512]{2,1,0:T(8,128)(2,1)S(1)} %collective-permute-done.5.rest_2_, ...), custom_call_target="tpu_custom_call" | custom-call | flops 268435456 | bytes 1048576 | tf_op jit(solution)/shard_map/lags/pallas_call | solution.py:310
  29.3 3.1 %collective-permute-done.3.rest_3_ = bf16[8,32,512]{2,1,0:T(8,128)(2,1)S(1)} collective-permute-done((bf16[8,32,512]{2,1,0:T(8,128)(2,1)S(1)}, bf16[8,32,512]{2,1,0:T(8,128)(2,1)S(1)}, u32[]{:S(2)}, u32[]{:S(2)}) %collective-permute-start.3) | collective-permute-done | bytes 262176 | tf_op jit(solution)/shard_map/ppermute | solution.py:286
  32.4 1.2 %lags.3 = bf16[8,64,512]{2,1,0:T(8,128)(2,1)} custom-call(bf16[512,512]{1,0:T(8,128)(2,1)S(1)} %get-tuple-element.13.table_ref, bf16[8,32,512]{2,1,0:T(8,128)(2,1)S(1)} %get-tuple-element.18.rest_0_, bf16[8,32,512]{2,1,0:T(8,128)(2,1)S(1)} %collective-permute-done.refs_0_.rest_1_, ...), custom_call_target="tpu_custom_call", output_to_operand_aliasing={{}: (5, {})} | custom-call | flops 268435456 | bytes 1048576 | tf_op jit(solution)/shard_map/lags/pallas_call | solution.py:310
Async XLA Ops:
  0.0 3.4 %copy-start = (bf16[64,8,512]{2,1,0:T(8,128)(2,1)S(1)}, bf16[64,8,512]{2,1,0:T(8,128)(2,1)}, u32[]{:S(2)}) copy-start(bf16[64,8,512]{2,1,0:T(8,128)(2,1)} %param.3) | copy-start | bytes 1572868
  1.5 8.1 %collective-permute-start.2 = (bf16[32,4096]{1,0:T(8,128)(2,1)S(1)}, bf16[32,4096]{1,0:T(8,128)(2,1)S(1)}, u32[]{:S(2)}, u32[]{:S(2)}) collective-permute-start(bf16[32,4096]{1,0:T(8,128)(2,1)S(1)} %get-tuple-element.17.edge_ref), channel_id=1, source_target_pairs={{4,0},{8,4},{12,8},{16,12},{20,16},{24,20},{28,24},{5,1},{9,5},{13... | collective-permute-start | bytes 786440 | tf_op jit(solution)/shard_map/ppermute | solution.py:257
  4.9 9.6 %collective-permute-start = (bf16[8,32,512]{2,1,0:T(8,128)(2,1)S(1)}, bf16[8,32,512]{2,1,0:T(8,128)(2,1)S(1)}, u32[]{:S(2)}, u32[]{:S(2)}) collective-permute-start(bf16[8,32,512]{2,1,0:T(8,128)(2,1)S(1)} %get-tuple-element.18.rest_0_), channel_id=1, source_target_pairs={{0,1},{1,3},{4,5},{5,7},{8,9},{9,11},{12,13},{13,15},{16,17},{17,1... | collective-permute-start | bytes 786440 | tf_op jit(solution)/shard_map/ppermute | solution.py:286
  5.6 17.2 %collective-permute-start.1 = (bf16[8,32,512]{2,1,0:T(8,128)(2,1)S(1)}, bf16[8,32,512]{2,1,0:T(8,128)(2,1)S(1)}, u32[]{:S(2)}, u32[]{:S(2)}) collective-permute-start(bf16[8,32,512]{2,1,0:T(8,128)(2,1)S(1)} %get-tuple-element.18.rest_0_), channel_id=1, source_target_pairs={{0,2},{2,3},{4,6},{6,7},{8,10},{10,11},{12,14},{14,15},{16,18},{18... | collective-permute-start | bytes 786440 | tf_op jit(solution)/shard_map/ppermute | solution.py:286
  10.6 14.2 %collective-permute-start.4 = (bf16[8,32,512]{2,1,0:T(8,128)(2,1)S(1)}, bf16[8,32,512]{2,1,0:T(8,128)(2,1)S(1)}, u32[]{:S(2)}, u32[]{:S(2)}) collective-permute-start(bf16[8,32,512]{2,1,0:T(8,128)(2,1)S(1)} %cross.1.refs_2_.rest_0_), channel_id=1, source_target_pairs={{0,3},{1,2},{4,7},{5,6},{8,11},{9,10},{12,15},{13,14},{16,19},{17,... | collective-permute-start | bytes 786440 | tf_op jit(solution)/shard_map/ppermute | solution.py:286
  11.9 12.9 %collective-permute-start.5 = (bf16[8,32,512]{2,1,0:T(8,128)(2,1)S(1)}, bf16[8,32,512]{2,1,0:T(8,128)(2,1)S(1)}, u32[]{:S(2)}, u32[]{:S(2)}) collective-permute-start(bf16[8,32,512]{2,1,0:T(8,128)(2,1)S(1)} %cross.1.refs_2_.rest_0_), channel_id=1, source_target_pairs={{0,1},{1,3},{4,5},{5,7},{8,9},{9,11},{12,13},{13,15},{16,17},{17,1... | collective-permute-start | bytes 786440 | tf_op jit(solution)/shard_map/ppermute | solution.py:286
  12.6 15.4 %collective-permute-start.6 = (bf16[8,32,512]{2,1,0:T(8,128)(2,1)S(1)}, bf16[8,32,512]{2,1,0:T(8,128)(2,1)S(1)}, u32[]{:S(2)}, u32[]{:S(2)}) collective-permute-start(bf16[8,32,512]{2,1,0:T(8,128)(2,1)S(1)} %cross.1.refs_2_.rest_0_), channel_id=1, source_target_pairs={{0,2},{2,3},{4,6},{6,7},{8,10},{10,11},{12,14},{14,15},{16,18},{18... | collective-permute-start | bytes 786440 | tf_op jit(solution)/shard_map/ppermute | solution.py:286
  22.9 9.5 %collective-permute-start.3 = (bf16[8,32,512]{2,1,0:T(8,128)(2,1)S(1)}, bf16[8,32,512]{2,1,0:T(8,128)(2,1)S(1)}, u32[]{:S(2)}, u32[]{:S(2)}) collective-permute-start(bf16[8,32,512]{2,1,0:T(8,128)(2,1)S(1)} %mix.1), channel_id=1, source_target_pairs={{2,3},{3,2},{6,7},{7,6},{10,11},{11,10},{14,15},{15,14},{18,19},{1... | collective-permute-start | bytes 786440 | tf_op jit(solution)/shard_map/ppermute | solution.py:286
where the time goes:
time: 34.2 us; the launch traced here: 33.6 us
  waiting for transfers between devices  14.5 us (42%)
  starting transfers between devices  12.4 us (36%)
  Pallas kernels  6.51 us (19%)
    ppermute x6, waiting for transfers between devices, sent(): return lax.ppermute(value, 'tm', moves)  14.5 us
    ppermute x6, starting transfers between devices, sent(): return lax.ppermute(value, 'tm', moves)  10.5 us
    pallas_call x2, Pallas kernels, lags(): pl.pallas_call(functools.partial(lag_kernel, bins ** (-0.5), first, weigh...  2.47 us
    ppermute x1, starting transfers between devices, per_device(): edge = lax.ppermute(short_a, 'chan', [(i, i - 1) for i in range(1, ring)])  1.92 us
    pallas_call x1, Pallas kernels, per_device(): pl.pallas_call(head_kernel, out_shape=(white_type, short_type, jax.ShapeD...  1.5 us
    pallas_call x1, Pallas kernels, per_device(): pl.pallas_call(tail_kernel, out_shape=(white_type, short_type, local_type...  1.45 us
    pallas_call x1, Pallas kernels, per_device(): pl.pallas_call(cross_kernel, out_shape=local_type, in_specs=[whole()] * 4...  0.99 us
  transfers between devices with their start and end apart: 7, of which 3 were waited for; matrix products, arithmetic and copies ran while one was open for 0% of the time, Pallas kernels for 11%

commit v1 on v0

--- a/solution.py
+++ b/solution.py
@@ -176,15 +176,19 @@
     return total
 
 
+def whereabouts(groups):
+    return lax.rem(lax.axis_index("chan"), 2) * groups + lax.axis_index("tm")
+
+
 def mix_kernel(weights, *refs):
-    place = lax.axis_index("tm")
+    place = whereabouts(len(weights[0]) // 2)
     total = weighted(refs[: len(weights)], weights, place)
     refs[-1][...] = total.astype(refs[-1].dtype)
 
 
 def lag_kernel(scale, first, weights, table_ref, *rest):
     out_hbm, stage_ref, sems = rest[-3:]
-    place = lax.axis_index("tm")
+    place = whereabouts(len(weights[0]) // 2)
     dims = (((1,), (1,)), ((), ()))
     pairs, rows, length = stage_ref.shape
     refs = rest[: len(weights)]
@@ -282,18 +286,13 @@
     columns = min(d for d in range(1, groups + 1) if groups % d == 0 and d * d >= groups)
     square = columns == 2 and groups == columns * columns
 
-    def sent(value, moves):
-        return lax.ppermute(value, "tm", moves)
-
-    def faded(moves):
-        origin = {there: here for here, there in moves}
-        return [power[h - origin[h]] if h in origin else 0.0 for h in range(groups)]
-
-    if square:
-        low, high = [(0, 1), (1, 3)], [(0, 2), (2, 3)]
-        straight = [[(0, 3), (1, 2)], low, high]
-    else:
-        straight = [[(h, h + d) for h in range(groups - d)] for d in range(1, groups)]
+    def sent(value, even, odd):
+        moves = [
+            (c * groups + here, c * groups + there)
+            for c in range(ring)
+            for here, there in (odd if c % 2 else even)
+        ]
+        return lax.ppermute(value, ("chan", "tm"), moves)
 
     def mix(terms, weights, after):
         return pl.pallas_call(
@@ -322,19 +321,35 @@
             name="lags",
         )(table, *terms, *so_far)
 
-    unit = [1.0] * groups
-    terms_b = [local_b] + [sent(local_b, moves) for moves in straight]
-    weights_b = [unit] + [faded(moves) for moves in straight]
-    if square:
-        got_low, got_high = sent(local_a, low), sent(local_a, high)
-        onward = mix([got_low, got_high], [[0.0, 0.0, 0.0, 1.0], [0.0, 0.0, 1.0, 0.0]], local_b)
-        terms_a = [local_a, got_low, got_high, sent(onward, [(2, 3), (3, 2)])]
-        weights_a = [unit, faded(low), faded(high), [0.0, 0.0, power[1], power[3]]]
-    else:
-        terms_a = [local_a] + [sent(local_a, moves) for moves in straight]
-        weights_a = weights_b
-    result = lags(half, terms_b, weights_b)
-    result = lags(0, terms_a, weights_a, result)
+    unit = [1.0] * (2 * groups)
+
+    def two_hops(local, after):
+        f, ff = power[1], power[2]
+        got = sent(local, [(0, 2), (1, 3)], [(0, 1), (1, 0), (2, 3)])
+        total = mix(
+            [local, got],
+            [[1.0, 1.0, 1.0, 0.0, f, 1.0, 0.0, 0.0], [ff, ff, ff, 1.0, 1.0, f, 0.0, 0.0]],
+            after,
+        )
+        more = sent(total, [(0, 1), (2, 3), (3, 2)], [(0, 2), (1, 3)])
+        weights = [
+            unit,
+            [ff, ff, ff, ff, 0.0, f, 0.0, f],
+            [f, f, f, f, 0.0, 0.0, f, ff],
+        ]
+        return [local, got, more], weights
+
+    def one_hop(local, after):
+        terms, weights = [local], [unit]
+        for d in range(1, groups):
+            moves = [(h, h + d) for h in range(groups - d)]
+            terms.append(sent(local, moves, moves))
+            weights.append([power[d]] * (2 * groups))
+        return terms, weights
+
+    spread = two_hops if square else one_hop
+    result = lags(0, *spread(local_a, local_b))
+    result = lags(half, *spread(local_b, local_b), result)
     return result.reshape(1, pairs, chans, length)
 
 

time: 34.2 us -> 26.5 us (0.77); the launches traced: 33.6 us -> 26.3 us
  waiting for transfers between devices: 14.5 us -> 8.46 us
  starting transfers between devices: 12.4 us -> 11.2 us
    ppermute x6 -> x4, waiting for transfers between devices: 14.5 us -> 7.35 us  [sent(): return lax.ppermute(value, ('chan', 'tm'), moves)]
    ppermute x6 -> x4, starting transfers between devices: 10.5 us -> 9.25 us  [sent(): return lax.ppermute(value, ('chan', 'tm'), moves)]
    ppermute x1, waiting for transfers between devices: 0.01 us -> 1.11 us  [per_device(): edge = lax.ppermute(short_a, 'chan', [(i, i - 1) for i in range(1, ring)])]
  transfers between devices with their start and end apart: 7 -> 5, of which waited for: 3 -> 4; matrix products, arithmetic and copies ran while one was open for 0% -> 0% of each run, Pallas kernels for 11% -> 15%
where the time goes in v1:
time: 26.5 us; the launch traced here: 26.3 us
  starting transfers between devices  11.2 us (42%)
  waiting for transfers between devices  8.46 us (32%)
  Pallas kernels  6.55 us (25%)
    ppermute x4, starting transfers between devices, sent(): return lax.ppermute(value, ('chan', 'tm'), moves)  9.25 us
    ppermute x4, waiting for transfers between devices, sent(): return lax.ppermute(value, ('chan', 'tm'), moves)  7.35 us
    pallas_call x2, Pallas kernels, lags(): pl.pallas_call(functools.partial(lag_kernel, bins ** (-0.5), first, weigh...  2.38 us
    ppermute x1, starting transfers between devices, per_device(): edge = lax.ppermute(short_a, 'chan', [(i, i - 1) for i in range(1, ring)])  1.92 us
    pallas_call x1, Pallas kernels, per_device(): pl.pallas_call(head_kernel, out_shape=(white_type, short_type, jax.ShapeD...  1.5 us
    pallas_call x1, Pallas kernels, per_device(): pl.pallas_call(tail_kernel, out_shape=(white_type, short_type, local_type...  1.45 us
    ppermute x1, waiting for transfers between devices, per_device(): edge = lax.ppermute(short_a, 'chan', [(i, i - 1) for i in range(1, ring)])  1.11 us
    pallas_call x1, Pallas kernels, per_device(): pl.pallas_call(cross_kernel, out_shape=local_type, in_specs=[whole()] * 4...  0.99 us
  transfers between devices with their start and end apart: 5, of which 4 were waited for; matrix products, arithmetic and copies ran while one was open for 0% of the time, Pallas kernels for 15%

profile of v1, /device:TPU:28, one launch (start us, length us, event | category | flops | bytes accessed | tf_op | source)
XLA Modules:
  0.0 26.3 jit_solution(15866369318382805886)
XLA Ops:
  0.0 0.0 copy-start
  0.0 1.5 %head.1 = (f32[8,32,512]{2,1,0:T(8,128)S(1)}, bf16[32,4096]{1,0:T(8,128)(2,1)S(1)}, bf16[512,512]{1,0:T(8,128)(2,1)S(1)}, bf16[8,32,64]{2,1,0:T(8,128)(2,1)S(1)}, f32[64,1024]{1,0:T(8,128)S(1)}) custom-call(bf16[512,512]{1,0:T(8,128)(2,1)} %bitcast.3, s32[8,64]{1,0:T(8,128)} %bitcast.5, s32[8]{0:T(128)} %offsets_hbm.1), custom_call_target="tpu_custom_call" | custom-call | flops 134217728 | bytes 2097152 | tf_op jit(solution)/shard_map/head/pallas_call | solution.py:237
  1.5 1.9 %collective-permute-start = (bf16[32,4096]{1,0:T(8,128)(2,1)S(1)}, bf16[32,4096]{1,0:T(8,128)(2,1)S(1)}, u32[]{:S(2)}, u32[]{:S(2)}) collective-permute-start(bf16[32,4096]{1,0:T(8,128)(2,1)S(1)} %get-tuple-element.17.edge_ref), channel_id=1, source_target_pairs={{4,0},{8,4},{12,8},{16,12},{20,16},{24,20},{28,24},{5,1},{9,5},{13... | collective-permute-start | bytes 786440 | tf_op jit(solution)/shard_map/ppermute | solution.py:261
  3.4 0.0 copy-done
  3.5 1.4 %tail.1 = (f32[8,32,512]{2,1,0:T(8,128)S(1)}, bf16[32,4096]{1,0:T(8,128)(2,1)S(1)}, bf16[8,32,512]{2,1,0:T(8,128)(2,1)S(1)}) custom-call(bf16[512,512]{1,0:T(8,128)(2,1)S(1)} %bitcast.4, bf16[512,512]{1,0:T(8,128)(2,1)S(1)} %get-tuple-element.13.table_ref, f32[64,1024]{1,0:T(8,128)S(1)} %get-tuple-element.15.keep_ref, ...), custom_call_target="tpu_custom_call" | custom-call | flops 268435456 | bytes 4194304 | tf_op jit(solution)/shard_map/tail/pallas_call | solution.py:263
  4.9 1.3 %collective-permute-start.3 = (bf16[8,32,512]{2,1,0:T(8,128)(2,1)S(1)}, bf16[8,32,512]{2,1,0:T(8,128)(2,1)S(1)}, u32[]{:S(2)}, u32[]{:S(2)}) collective-permute-start(bf16[8,32,512]{2,1,0:T(8,128)(2,1)S(1)} %get-tuple-element.20.refs_0_.rest_0_), channel_id=1, source_target_pairs={{0,2},{1,3},{4,5},{5,4},{6,7},{8,10},{9,11},{12,13},{13,12},{14,15... | collective-permute-start | bytes 786440 | tf_op jit(solution)/shard_map/ppermute | solution.py:295
  6.2 1.1 %collective-permute-done.edge_ref = bf16[32,4096]{1,0:T(8,128)(2,1)S(1)} collective-permute-done((bf16[32,4096]{1,0:T(8,128)(2,1)S(1)}, bf16[32,4096]{1,0:T(8,128)(2,1)S(1)}, u32[]{:S(2)}, u32[]{:S(2)}) %collective-permute-start) | collective-permute-done | bytes 262176 | tf_op jit(solution)/shard_map/ppermute | solution.py:261
  7.3 1.0 %cross.1.refs_0_.refs_2_.rest_0_ = bf16[8,32,512]{2,1,0:T(8,128)(2,1)S(1)} custom-call(bf16[8,32,64]{2,1,0:T(8,128)(2,1)S(1)} %get-tuple-element.14.pick_ref, f32[8,32,512]{2,1,0:T(8,128)S(1)} %get-tuple-element.18.white_ref, bf16[32,4096]{1,0:T(8,128)(2,1)S(1)} %get-tuple-element.19.short_ref, bf16[32,4096]{1,0:T(8,128)(2,1)S(1)} %collective-permute-done.edge_ref), custom_call_target="tpu_custom_call" | custom-call | flops 4194304 | bytes 4194304 | tf_op jit(solution)/shard_map/cross/pallas_call | solution.py:274
  8.3 1.3 %collective-permute-start.1 = (bf16[8,32,512]{2,1,0:T(8,128)(2,1)S(1)}, bf16[8,32,512]{2,1,0:T(8,128)(2,1)S(1)}, u32[]{:S(2)}, u32[]{:S(2)}) collective-permute-start(bf16[8,32,512]{2,1,0:T(8,128)(2,1)S(1)} %cross.1.refs_0_.refs_2_.rest_0_), channel_id=1, source_target_pairs={{0,2},{1,3},{4,5},{5,4},{6,7},{8,10},{9,11},{12,13},{13,12},{14,15... | collective-permute-start | bytes 786440 | tf_op jit(solution)/shard_map/ppermute | solution.py:295
  9.6 3.6 %collective-permute-done.3.refs_1_.rest_1_ = bf16[8,32,512]{2,1,0:T(8,128)(2,1)S(1)} collective-permute-done((bf16[8,32,512]{2,1,0:T(8,128)(2,1)S(1)}, bf16[8,32,512]{2,1,0:T(8,128)(2,1)S(1)}, u32[]{:S(2)}, u32[]{:S(2)}) %collective-permute-start.3) | collective-permute-done | bytes 262176 | tf_op jit(solution)/shard_map/ppermute | solution.py:295
  13.2 0.1 mix.3
  13.3 3.4 %collective-permute-start.4 = (bf16[8,32,512]{2,1,0:T(8,128)(2,1)S(1)}, bf16[8,32,512]{2,1,0:T(8,128)(2,1)S(1)}, u32[]{:S(2)}, u32[]{:S(2)}) collective-permute-start(bf16[8,32,512]{2,1,0:T(8,128)(2,1)S(1)} %mix.3), channel_id=1, source_target_pairs={{0,1},{2,3},{3,2},{4,6},{5,7},{8,9},{10,11},{11,10},{12,14},{13,15... | collective-permute-start | bytes 786440 | tf_op jit(solution)/shard_map/ppermute | solution.py:295
  16.7 0.0 collective-permute-done.1.refs_1_.rest_1_
  16.7 0.1 mix.2
  16.8 3.3 %collective-permute-start.2 = (bf16[8,32,512]{2,1,0:T(8,128)(2,1)S(1)}, bf16[8,32,512]{2,1,0:T(8,128)(2,1)S(1)}, u32[]{:S(2)}, u32[]{:S(2)}) collective-permute-start(bf16[8,32,512]{2,1,0:T(8,128)(2,1)S(1)} %mix.2), channel_id=1, source_target_pairs={{0,1},{2,3},{3,2},{4,6},{5,7},{8,9},{10,11},{11,10},{12,14},{13,15... | collective-permute-start | bytes 786440 | tf_op jit(solution)/shard_map/ppermute | solution.py:295
  20.1 1.4 %collective-permute-done.4.rest_2_ = bf16[8,32,512]{2,1,0:T(8,128)(2,1)S(1)} collective-permute-done((bf16[8,32,512]{2,1,0:T(8,128)(2,1)S(1)}, bf16[8,32,512]{2,1,0:T(8,128)(2,1)S(1)}, u32[]{:S(2)}, u32[]{:S(2)}) %collective-permute-start.4) | collective-permute-done | bytes 262176 | tf_op jit(solution)/shard_map/ppermute | solution.py:295
  21.6 1.2 %lags.2.rest_3_ = bf16[8,64,512]{2,1,0:T(8,128)(2,1)} custom-call(bf16[512,512]{1,0:T(8,128)(2,1)S(1)} %get-tuple-element.13.table_ref, bf16[8,32,512]{2,1,0:T(8,128)(2,1)S(1)} %get-tuple-element.20.refs_0_.rest_0_, bf16[8,32,512]{2,1,0:T(8,128)(2,1)S(1)} %collective-permute-done.3.refs_1_.rest_1_, bf16[8,32,512]{2,1,0:T(8,128)(2,1)S(1)} %collective-permute-done.4.rest_2_), custom_call_target="tpu_custom_call" | custom-call | flops 268435456 | bytes 1048576 | tf_op jit(solution)/shard_map/lags/pallas_call | solution.py:309
  22.8 2.3 %collective-permute-done.2.rest_2_ = bf16[8,32,512]{2,1,0:T(8,128)(2,1)S(1)} collective-permute-done((bf16[8,32,512]{2,1,0:T(8,128)(2,1)S(1)}, bf16[8,32,512]{2,1,0:T(8,128)(2,1)S(1)}, u32[]{:S(2)}, u32[]{:S(2)}) %collective-permute-start.2) | collective-permute-done | bytes 262176 | tf_op jit(solution)/shard_map/ppermute | solution.py:295
  25.1 1.2 %lags.3 = bf16[8,64,512]{2,1,0:T(8,128)(2,1)} custom-call(bf16[512,512]{1,0:T(8,128)(2,1)S(1)} %get-tuple-element.13.table_ref, bf16[8,32,512]{2,1,0:T(8,128)(2,1)S(1)} %cross.1.refs_0_.refs_2_.rest_0_, bf16[8,32,512]{2,1,0:T(8,128)(2,1)S(1)} %collective-permute-done.1.refs_1_.rest_1_, ...), custom_call_target="tpu_custom_call", output_to_operand_aliasing={{}: (4, {})} | custom-call | flops 268435456 | bytes 1048576 | tf_op jit(solution)/shard_map/lags/pallas_call | solution.py:309
Async XLA Ops:
  0.0 3.4 %copy-start = (bf16[64,8,512]{2,1,0:T(8,128)(2,1)S(1)}, bf16[64,8,512]{2,1,0:T(8,128)(2,1)}, u32[]{:S(2)}) copy-start(bf16[64,8,512]{2,1,0:T(8,128)(2,1)} %param.3) | copy-start | bytes 1572868
  1.5 5.8 %collective-permute-start = (bf16[32,4096]{1,0:T(8,128)(2,1)S(1)}, bf16[32,4096]{1,0:T(8,128)(2,1)S(1)}, u32[]{:S(2)}, u32[]{:S(2)}) collective-permute-start(bf16[32,4096]{1,0:T(8,128)(2,1)S(1)} %get-tuple-element.17.edge_ref), channel_id=1, source_target_pairs={{4,0},{8,4},{12,8},{16,12},{20,16},{24,20},{28,24},{5,1},{9,5},{13... | collective-permute-start | bytes 786440 | tf_op jit(solution)/shard_map/ppermute | solution.py:261
  4.9 8.3 %collective-permute-start.3 = (bf16[8,32,512]{2,1,0:T(8,128)(2,1)S(1)}, bf16[8,32,512]{2,1,0:T(8,128)(2,1)S(1)}, u32[]{:S(2)}, u32[]{:S(2)}) collective-permute-start(bf16[8,32,512]{2,1,0:T(8,128)(2,1)S(1)} %get-tuple-element.20.refs_0_.rest_0_), channel_id=1, source_target_pairs={{0,2},{1,3},{4,5},{5,4},{6,7},{8,10},{9,11},{12,13},{13,12},{14,15... | collective-permute-start | bytes 786440 | tf_op jit(solution)/shard_map/ppermute | solution.py:295
  8.3 8.4 %collective-permute-start.1 = (bf16[8,32,512]{2,1,0:T(8,128)(2,1)S(1)}, bf16[8,32,512]{2,1,0:T(8,128)(2,1)S(1)}, u32[]{:S(2)}, u32[]{:S(2)}) collective-permute-start(bf16[8,32,512]{2,1,0:T(8,128)(2,1)S(1)} %cross.1.refs_0_.refs_2_.rest_0_), channel_id=1, source_target_pairs={{0,2},{1,3},{4,5},{5,4},{6,7},{8,10},{9,11},{12,13},{13,12},{14,15... | collective-permute-start | bytes 786440 | tf_op jit(solution)/shard_map/ppermute | solution.py:295
  13.3 8.3 %collective-permute-start.4 = (bf16[8,32,512]{2,1,0:T(8,128)(2,1)S(1)}, bf16[8,32,512]{2,1,0:T(8,128)(2,1)S(1)}, u32[]{:S(2)}, u32[]{:S(2)}) collective-permute-start(bf16[8,32,512]{2,1,0:T(8,128)(2,1)S(1)} %mix.3), channel_id=1, source_target_pairs={{0,1},{2,3},{3,2},{4,6},{5,7},{8,9},{10,11},{11,10},{12,14},{13,15... | collective-permute-start | bytes 786440 | tf_op jit(solution)/shard_map/ppermute | solution.py:295
  16.8 8.3 %collective-permute-start.2 = (bf16[8,32,512]{2,1,0:T(8,128)(2,1)S(1)}, bf16[8,32,512]{2,1,0:T(8,128)(2,1)S(1)}, u32[]{:S(2)}, u32[]{:S(2)}) collective-permute-start(bf16[8,32,512]{2,1,0:T(8,128)(2,1)S(1)} %mix.2), channel_id=1, source_target_pairs={{0,1},{2,3},{3,2},{4,6},{5,7},{8,9},{10,11},{11,10},{12,14},{13,15... | collective-permute-start | bytes 786440 | tf_op jit(solution)/shard_map/ppermute | solution.py:295

commit v2 on v1

--- a/solution.py
+++ b/solution.py
@@ -41,6 +41,27 @@
         cos_i, sin_i = coarse_cos[i : i + 1], coarse_sin[i : i + 1]
         table_ref[rows, :bins] = (cos_i * fine_cos - sin_i * fine_sin).astype(jnp.bfloat16)
         table_ref[rows, bins:] = -(sin_i * fine_cos + cos_i * fine_sin).astype(jnp.bfloat16)
+
+
+def inverse_kernel(_, table_ref):
+    length = table_ref.shape[0]
+    bins = length // 2
+    step = 16
+
+    def small(rows, by, first):
+        freq = (lax.broadcasted_iota(jnp.int32, (rows, length), 0) + first) * by
+        lag = lax.broadcasted_iota(jnp.int32, (rows, length), 1)
+        return turns((freq * lag).astype(jnp.float32), length)
+
+    coarse_cos, coarse_sin = small(bins // step, step, 0)
+    fine_cos, fine_sin = small(step, 1, 1)
+    for i in range(bins // step):
+        first = i * step
+        cos_i, sin_i = coarse_cos[i : i + 1], coarse_sin[i : i + 1]
+        cosine = cos_i * fine_cos - sin_i * fine_sin
+        sine = sin_i * fine_cos + cos_i * fine_sin
+        table_ref[first : first + step, :] = cosine.astype(jnp.bfloat16)
+        table_ref[bins + first : bins + first + step, :] = (-sine).astype(jnp.bfloat16)
 
 
 def whiten_block(x, table, keep, raw_ref, white_ref, short_ref):
@@ -84,32 +105,31 @@
 ):
     wins, span, length = white_ref.shape
     pairs = offsets_ref.shape[0]
-    copies = [
-        pltpu.make_async_copy(valid_hbm, valid_ref, sems.at[0]),
-        pltpu.make_async_copy(offsets_hbm, offsets_ref, sems.at[1]),
-        pltpu.make_async_copy(x_hbm.at[pl.ds(0, span * wins)], x_ref, sems.at[2]),
-    ]
-    for copy in copies:
+    valid_copy = pltpu.make_async_copy(valid_hbm, valid_ref, sems.at[0])
+    x_copy = pltpu.make_async_copy(x_hbm.at[pl.ds(0, span * wins)], x_ref, sems.at[1])
+    offsets_copy = pltpu.make_async_copy(offsets_hbm, offsets_ref, sems.at[2])
+    for copy in (x_copy, valid_copy, offsets_copy):
         copy.start()
     fill_table(table_ref, 16)
-    copies[0].wait()
-    copies[1].wait()
+    owner = lax.broadcasted_iota(jnp.int32, (wins, wins * LANES), 0)
+    column = lax.broadcasted_iota(jnp.int32, (wins, wins * LANES), 1) // LANES
+    mine = (owner == column).astype(jnp.float32).astype(jnp.bfloat16)
+    valid_copy.wait()
+    keep_ref[...] = lax.dot_general(
+        valid_ref[...].astype(jnp.float32).astype(jnp.bfloat16),
+        mine,
+        (((0,), (0,)), ((), ())),
+        preferred_element_type=jnp.float32,
+    )
+    x_copy.wait()
+    whiten_block(x_ref[...], table_ref[...], keep_ref[:span], raw_ref, white_ref, short_ref)
+    offsets_copy.wait()
     ahead = lax.broadcasted_iota(jnp.int32, (span, 2 * span), 1) - lax.broadcasted_iota(
         jnp.int32, (span, 2 * span), 0
     )
     for k in range(pairs):
-        chosen_row = jnp.where(ahead == offsets_ref[k], jnp.float32(1.0), jnp.float32(0.0))
-        pick_ref[k] = chosen_row.astype(jnp.bfloat16)
-    owner = lax.broadcasted_iota(jnp.int32, (wins, wins * LANES), 0)
-    column = lax.broadcasted_iota(jnp.int32, (wins, wins * LANES), 1) // LANES
-    keep_ref[...] = lax.dot_general(
-        valid_ref[...].astype(jnp.float32).astype(jnp.bfloat16),
-        (owner == column).astype(jnp.float32).astype(jnp.bfloat16),
-        (((0,), (0,)), ((), ())),
-        preferred_element_type=jnp.float32,
-    )
-    copies[2].wait()
-    whiten_block(x_ref[...], table_ref[...], keep_ref[:span], raw_ref, white_ref, short_ref)
+        row = jnp.where(ahead == offsets_ref[k], jnp.float32(1.0), jnp.float32(0.0))
+        pick_ref[k] = row.astype(jnp.bfloat16)
 
 
 def stack_pairs(pick_ref, white_ref, near_ref, parts_ref, out_ref):
@@ -189,19 +209,23 @@
 def lag_kernel(scale, first, weights, table_ref, *rest):
     out_hbm, stage_ref, sems = rest[-3:]
     place = whereabouts(len(weights[0]) // 2)
-    dims = (((1,), (1,)), ((), ()))
     pairs, rows, length = stage_ref.shape
-    refs = rest[: len(weights)]
-    stack = weighted(refs, weights, place).reshape(pairs * rows, length)
+    count = pairs * rows
+    stack = weighted(rest[: len(weights)], weights, place).reshape(count, length)
     high = stack.astype(jnp.bfloat16)
     low = (stack - high.astype(jnp.float32)).astype(jnp.bfloat16)
-    table = table_ref[...]
-    lagged = lax.dot_general(high, table, dims, preferred_element_type=jnp.float32)
-    lagged = lagged + lax.dot_general(low, table, dims, preferred_element_type=jnp.float32)
-    stage_ref[...] = (lagged * scale).astype(stage_ref.dtype).reshape(pairs, rows, length)
-    copy = pltpu.make_async_copy(stage_ref, out_hbm.at[:, pl.ds(first, rows)], sems.at[0])
-    copy.start()
-    copy.wait()
+    both = jnp.concatenate([high, low], axis=0)
+    copies = []
+    for half in range(2):
+        lanes = pl.ds(half * length // 2, length // 2)
+        lagged = jnp.dot(both, table_ref[:, lanes], preferred_element_type=jnp.float32)
+        lagged = (lagged[:count] + lagged[count:]) * scale
+        stage_ref[:, :, lanes] = lagged.astype(stage_ref.dtype).reshape(pairs, rows, length // 2)
+        there = out_hbm.at[:, pl.ds(first, rows), lanes]
+        copies.append(pltpu.make_async_copy(stage_ref.at[:, :, lanes], there, sems.at[half]))
+        copies[-1].start()
+    for copy in copies:
+        copy.wait()
 
 
 def cost(flops, moved):
@@ -305,27 +329,40 @@
             name="mix",
         )(*terms, after)
 
-    def lags(first, terms, weights, *so_far):
+    inverse = pl.pallas_call(
+        inverse_kernel,
+        out_shape=jax.ShapeDtypeStruct((length, length), jnp.bfloat16),
+        in_specs=[whole(pl.ANY)],
+        out_specs=whole(),
+        compiler_params=params,
+        cost_estimate=cost(length * bins * 32, 512 * 1024),
+        name="inverse",
+    )(local_b)
+
+    def lags(first, terms, weights, later, *so_far):
+        so_far = list(so_far)
         return pl.pallas_call(
             functools.partial(lag_kernel, bins**-0.5, first, weights),
             out_shape=jax.ShapeDtypeStruct((pairs, chans, length), jnp.bfloat16),
-            in_specs=[whole()] * (1 + len(terms)) + [whole(pl.ANY)] * len(so_far),
+            in_specs=[whole()] * (1 + len(terms)) + [whole(pl.ANY)] * len(later + so_far),
             out_specs=whole(pl.ANY),
             scratch_shapes=[
                 pltpu.VMEM((pairs, span, length), jnp.bfloat16),
-                pltpu.SemaphoreType.DMA((1,)),
+                pltpu.SemaphoreType.DMA((2,)),
             ],
-            input_output_aliases={1 + len(terms): 0} if so_far else {},
+            input_output_aliases={1 + len(terms + later): 0} if so_far else {},
             compiler_params=params,
             cost_estimate=cost(pairs * span * length * length * 4, 1024 * 1024),
             name="lags",
-        )(table, *terms, *so_far)
+        )(inverse, *terms, *later, *so_far)
 
     unit = [1.0] * (2 * groups)
 
-    def two_hops(local, after):
+    def two_hops(local, after, apart):
         f, ff = power[1], power[2]
-        got = sent(local, [(0, 2), (1, 3)], [(0, 1), (1, 0), (2, 3)])
+        last = [(2, 3)]
+        got = sent(local, [(0, 2), (1, 3)], [(0, 1), (1, 0)] + ([] if apart else last))
+        alone = [sent(local, [], last)] if apart else []
         total = mix(
             [local, got],
             [[1.0, 1.0, 1.0, 0.0, f, 1.0, 0.0, 0.0], [ff, ff, ff, 1.0, 1.0, f, 0.0, 0.0]],
@@ -336,10 +373,10 @@
             unit,
             [ff, ff, ff, ff, 0.0, f, 0.0, f],
             [f, f, f, f, 0.0, 0.0, f, ff],
-        ]
-        return [local, got, more], weights
-
-    def one_hop(local, after):
+        ] + [[f] * (2 * groups)] * len(alone)
+        return [local, got, more] + alone, weights
+
+    def one_hop(local, after, apart):
         terms, weights = [local], [unit]
         for d in range(1, groups):
             moves = [(h, h + d) for h in range(groups - d)]
@@ -348,8 +385,10 @@
         return terms, weights
 
     spread = two_hops if square else one_hop
-    result = lags(0, *spread(local_a, local_b))
-    result = lags(half, *spread(local_b, local_b), result)
+    terms_a, weights_a = spread(local_a, local_b, False)
+    terms_b, weights_b = spread(local_b, local_b, True)
+    result = lags(0, terms_a, weights_a, terms_b[3:4])
+    result = lags(half, terms_b, weights_b, [], result)
     return result.reshape(1, pairs, chans, length)
 
 

time: 26.5 us -> 29 us (1.094)
  the two profiles are of different devices: /device:TPU:28 before, /device:TPU:30 now
where the time goes in v2:
time: 29 us; the launch traced here: 28.7 us
  starting transfers between devices  10.9 us (38%)
  waiting for transfers between devices  10.2 us (35%)
  Pallas kernels  7.54 us (26%)
    ppermute x5, waiting for transfers between devices, sent(): return lax.ppermute(value, ('chan', 'tm'), moves)  9.08 us
    ppermute x5, starting transfers between devices, sent(): return lax.ppermute(value, ('chan', 'tm'), moves)  8.96 us
    pallas_call x2, Pallas kernels, lags(): pl.pallas_call(functools.partial(lag_kernel, bins ** (-0.5), first, weigh...  3.03 us
    ppermute x1, starting transfers between devices, per_device(): edge = lax.ppermute(short_a, 'chan', [(i, i - 1) for i in range(1, ring)])  1.92 us
    pallas_call x1, Pallas kernels, per_device(): pl.pallas_call(head_kernel, out_shape=(white_type, short_type, jax.ShapeD...  1.55 us
    pallas_call x1, Pallas kernels, per_device(): pl.pallas_call(tail_kernel, out_shape=(white_type, short_type, local_type...  1.45 us
    ppermute x1, waiting for transfers between devices, per_device(): edge = lax.ppermute(short_a, 'chan', [(i, i - 1) for i in range(1, ring)])  1.11 us
    pallas_call x1, Pallas kernels, per_device(): pl.pallas_call(cross_kernel, out_shape=local_type, in_specs=[whole()] * 4...  1 us
  transfers between devices with their start and end apart: 6, of which 5 were waited for; matrix products, arithmetic and copies ran while one was open for 0% of the time, Pallas kernels for 16%

profile of v2, /device:TPU:30, one launch (start us, length us, event | category | flops | bytes accessed | tf_op | source)
XLA Modules:
  0.0 28.7 jit_solution(5375969280842115156)
XLA Ops:
  0.0 0.0 copy-start
  0.0 1.5 %head.1 = (f32[8,32,512]{2,1,0:T(8,128)S(1)}, bf16[32,4096]{1,0:T(8,128)(2,1)S(1)}, bf16[512,512]{1,0:T(8,128)(2,1)S(1)}, bf16[8,32,64]{2,1,0:T(8,128)(2,1)S(1)}, f32[64,1024]{1,0:T(8,128)S(1)}) custom-call(bf16[512,512]{1,0:T(8,128)(2,1)} %bitcast.3, s32[8,64]{1,0:T(8,128)} %bitcast.5, s32[8]{0:T(128)} %offsets_hbm.1), custom_call_target="tpu_custom_call" | custom-call | flops 134217728 | bytes 2097152 | tf_op jit(solution)/shard_map/head/pallas_call | solution.py:261
  1.6 1.9 %collective-permute-start = (bf16[32,4096]{1,0:T(8,128)(2,1)S(1)}, bf16[32,4096]{1,0:T(8,128)(2,1)S(1)}, u32[]{:S(2)}, u32[]{:S(2)}) collective-permute-start(bf16[32,4096]{1,0:T(8,128)(2,1)S(1)} %get-tuple-element.17.edge_ref), channel_id=1, source_target_pairs={{4,0},{8,4},{12,8},{16,12},{20,16},{24,20},{28,24},{5,1},{9,5},{13... | collective-permute-start | bytes 786440 | tf_op jit(solution)/shard_map/ppermute | solution.py:285
  3.5 0.0 copy-done
  3.5 1.4 %tail.1 = (f32[8,32,512]{2,1,0:T(8,128)S(1)}, bf16[32,4096]{1,0:T(8,128)(2,1)S(1)}, bf16[8,32,512]{2,1,0:T(8,128)(2,1)S(1)}) custom-call(bf16[512,512]{1,0:T(8,128)(2,1)S(1)} %bitcast.4, bf16[512,512]{1,0:T(8,128)(2,1)S(1)} %get-tuple-element.14.table_ref, f32[64,1024]{1,0:T(8,128)S(1)} %get-tuple-element.15.keep_ref, ...), custom_call_target="tpu_custom_call" | custom-call | flops 268435456 | bytes 4194304 | tf_op jit(solution)/shard_map/tail/pallas_call | solution.py:287
  4.9 1.3 %collective-permute-start.4 = (bf16[8,32,512]{2,1,0:T(8,128)(2,1)S(1)}, bf16[8,32,512]{2,1,0:T(8,128)(2,1)S(1)}, u32[]{:S(2)}, u32[]{:S(2)}) collective-permute-start(bf16[8,32,512]{2,1,0:T(8,128)(2,1)S(1)} %get-tuple-element.20.refs_0_.rest_0_), channel_id=1, source_target_pairs={{0,2},{1,3},{4,5},{5,4},{6,7},{8,10},{9,11},{12,13},{13,12},{14,15... | collective-permute-start | bytes 786440 | tf_op jit(solution)/shard_map/ppermute | solution.py:319
  6.2 1.1 %collective-permute-done.edge_ref = bf16[32,4096]{1,0:T(8,128)(2,1)S(1)} collective-permute-done((bf16[32,4096]{1,0:T(8,128)(2,1)S(1)}, bf16[32,4096]{1,0:T(8,128)(2,1)S(1)}, u32[]{:S(2)}, u32[]{:S(2)}) %collective-permute-start) | collective-permute-done | bytes 262176 | tf_op jit(solution)/shard_map/ppermute | solution.py:285
  7.4 1.0 %cross.1._.refs_0_.refs_2_.rest_0_ = bf16[8,32,512]{2,1,0:T(8,128)(2,1)S(1)} custom-call(bf16[8,32,64]{2,1,0:T(8,128)(2,1)S(1)} %get-tuple-element.13.pick_ref, f32[8,32,512]{2,1,0:T(8,128)S(1)} %get-tuple-element.18.white_ref, bf16[32,4096]{1,0:T(8,128)(2,1)S(1)} %get-tuple-element.19.short_ref, bf16[32,4096]{1,0:T(8,128)(2,1)S(1)} %collective-permute-done.edge_ref), custom_call_target="tpu_custom_call" | custom-call | flops 4194304 | bytes 4194304 | tf_op jit(solution)/shard_map/cross/pallas_call | solution.py:298
  8.4 1.3 %collective-permute-start.1 = (bf16[8,32,512]{2,1,0:T(8,128)(2,1)S(1)}, bf16[8,32,512]{2,1,0:T(8,128)(2,1)S(1)}, u32[]{:S(2)}, u32[]{:S(2)}) collective-permute-start(bf16[8,32,512]{2,1,0:T(8,128)(2,1)S(1)} %cross.1._.refs_0_.refs_2_.rest_0_), channel_id=1, source_target_pairs={{0,2},{1,3},{4,5},{5,4},{8,10},{9,11},{12,13},{13,12},{16,18},{17,... | collective-permute-start | bytes 786440 | tf_op jit(solution)/shard_map/ppermute | solution.py:319
  9.7 3.6 %collective-permute-done.4.refs_1_.rest_1_ = bf16[8,32,512]{2,1,0:T(8,128)(2,1)S(1)} collective-permute-done((bf16[8,32,512]{2,1,0:T(8,128)(2,1)S(1)}, bf16[8,32,512]{2,1,0:T(8,128)(2,1)S(1)}, u32[]{:S(2)}, u32[]{:S(2)}) %collective-permute-start.4) | collective-permute-done | bytes 262176 | tf_op jit(solution)/shard_map/ppermute | solution.py:319
  13.2 0.1 mix.3
  13.3 2.4 %collective-permute-start.5 = (bf16[8,32,512]{2,1,0:T(8,128)(2,1)S(1)}, bf16[8,32,512]{2,1,0:T(8,128)(2,1)S(1)}, u32[]{:S(2)}, u32[]{:S(2)}) collective-permute-start(bf16[8,32,512]{2,1,0:T(8,128)(2,1)S(1)} %mix.3), channel_id=1, source_target_pairs={{0,1},{2,3},{3,2},{4,6},{5,7},{8,9},{10,11},{11,10},{12,14},{13,15... | collective-permute-start | bytes 786440 | tf_op jit(solution)/shard_map/ppermute | solution.py:319
  15.8 0.7 %collective-permute-start.3 = (bf16[8,32,512]{2,1,0:T(8,128)(2,1)S(1)}, bf16[8,32,512]{2,1,0:T(8,128)(2,1)S(1)}, u32[]{:S(2)}, u32[]{:S(2)}) collective-permute-start(bf16[8,32,512]{2,1,0:T(8,128)(2,1)S(1)} %cross.1._.refs_0_.refs_2_.rest_0_), channel_id=1, source_target_pairs={{6,7},{14,15},{22,23},{30,31}} | collective-permute-start | bytes 786440 | tf_op jit(solution)/shard_map/ppermute | solution.py:319
  16.5 0.2 collective-permute-done.1.refs_1_.rest_1_
  16.6 0.1 mix.2
  16.7 3.3 %collective-permute-start.2 = (bf16[8,32,512]{2,1,0:T(8,128)(2,1)S(1)}, bf16[8,32,512]{2,1,0:T(8,128)(2,1)S(1)}, u32[]{:S(2)}, u32[]{:S(2)}) collective-permute-start(bf16[8,32,512]{2,1,0:T(8,128)(2,1)S(1)} %mix.2), channel_id=1, source_target_pairs={{0,1},{2,3},{3,2},{4,6},{5,7},{8,9},{10,11},{11,10},{12,14},{13,15... | collective-permute-start | bytes 786440 | tf_op jit(solution)/shard_map/ppermute | solution.py:319
  20.0 0.3 %inverse.1.table_ref = bf16[512,512]{1,0:T(8,128)(2,1)S(1)} custom-call(bf16[8,32,512]{2,1,0:T(8,128)(2,1)S(1)} %cross.1._.refs_0_.refs_2_.rest_0_), custom_call_target="tpu_custom_call" | custom-call | flops 4194304 | bytes 524288 | tf_op jit(solution)/shard_map/inverse/pallas_call | solution.py:332
  20.3 4.1 %collective-permute-done.5.rest_2_ = bf16[8,32,512]{2,1,0:T(8,128)(2,1)S(1)} collective-permute-done((bf16[8,32,512]{2,1,0:T(8,128)(2,1)S(1)}, bf16[8,32,512]{2,1,0:T(8,128)(2,1)S(1)}, u32[]{:S(2)}, u32[]{:S(2)}) %collective-permute-start.5) | collective-permute-done | bytes 262176 | tf_op jit(solution)/shard_map/ppermute | solution.py:319
  24.4 0.0 collective-permute-done.3.rest_3_
  24.4 1.5 %lags.2.rest_4_ = bf16[8,64,512]{2,1,0:T(8,128)(2,1)} custom-call(bf16[512,512]{1,0:T(8,128)(2,1)S(1)} %inverse.1.table_ref, bf16[8,32,512]{2,1,0:T(8,128)(2,1)S(1)} %get-tuple-element.20.refs_0_.rest_0_, bf16[8,32,512]{2,1,0:T(8,128)(2,1)S(1)} %collective-permute-done.4.refs_1_.rest_1_, bf16[8,32,512]{2,1,0:T(8,128)(2,1)S(1)} %collective-permute-done.5.rest_2_, ...), custom_call_target="tpu_custom_call" | custom-call | flops 268435456 | bytes 1048576 | tf_op jit(solution)/shard_map/lags/pallas_call | solution.py:344
  25.9 1.3 %collective-permute-done.2.rest_2_ = bf16[8,32,512]{2,1,0:T(8,128)(2,1)S(1)} collective-permute-done((bf16[8,32,512]{2,1,0:T(8,128)(2,1)S(1)}, bf16[8,32,512]{2,1,0:T(8,128)(2,1)S(1)}, u32[]{:S(2)}, u32[]{:S(2)}) %collective-permute-start.2) | collective-permute-done | bytes 262176 | tf_op jit(solution)/shard_map/ppermute | solution.py:319
  27.2 1.5 %lags.3 = bf16[8,64,512]{2,1,0:T(8,128)(2,1)} custom-call(bf16[512,512]{1,0:T(8,128)(2,1)S(1)} %inverse.1.table_ref, bf16[8,32,512]{2,1,0:T(8,128)(2,1)S(1)} %cross.1._.refs_0_.refs_2_.rest_0_, bf16[8,32,512]{2,1,0:T(8,128)(2,1)S(1)} %collective-permute-done.1.refs_1_.rest_1_, ...), custom_call_target="tpu_custom_call", output_to_operand_aliasing={{}: (5, {})} | custom-call | flops 268435456 | bytes 1048576 | tf_op jit(solution)/shard_map/lags/pallas_call | solution.py:344
Async XLA Ops:
  0.0 3.5 %copy-start = (bf16[64,8,512]{2,1,0:T(8,128)(2,1)S(1)}, bf16[64,8,512]{2,1,0:T(8,128)(2,1)}, u32[]{:S(2)}) copy-start(bf16[64,8,512]{2,1,0:T(8,128)(2,1)} %param.3) | copy-start | bytes 1572868
  1.6 5.8 %collective-permute-start = (bf16[32,4096]{1,0:T(8,128)(2,1)S(1)}, bf16[32,4096]{1,0:T(8,128)(2,1)S(1)}, u32[]{:S(2)}, u32[]{:S(2)}) collective-permute-start(bf16[32,4096]{1,0:T(8,128)(2,1)S(1)} %get-tuple-element.17.edge_ref), channel_id=1, source_target_pairs={{4,0},{8,4},{12,8},{16,12},{20,16},{24,20},{28,24},{5,1},{9,5},{13... | collective-permute-start | bytes 786440 | tf_op jit(solution)/shard_map/ppermute | solution.py:285
  4.9 8.3 %collective-permute-start.4 = (bf16[8,32,512]{2,1,0:T(8,128)(2,1)S(1)}, bf16[8,32,512]{2,1,0:T(8,128)(2,1)S(1)}, u32[]{:S(2)}, u32[]{:S(2)}) collective-permute-start(bf16[8,32,512]{2,1,0:T(8,128)(2,1)S(1)} %get-tuple-element.20.refs_0_.rest_0_), channel_id=1, source_target_pairs={{0,2},{1,3},{4,5},{5,4},{6,7},{8,10},{9,11},{12,13},{13,12},{14,15... | collective-permute-start | bytes 786440 | tf_op jit(solution)/shard_map/ppermute | solution.py:319
  8.4 8.3 %collective-permute-start.1 = (bf16[8,32,512]{2,1,0:T(8,128)(2,1)S(1)}, bf16[8,32,512]{2,1,0:T(8,128)(2,1)S(1)}, u32[]{:S(2)}, u32[]{:S(2)}) collective-permute-start(bf16[8,32,512]{2,1,0:T(8,128)(2,1)S(1)} %cross.1._.refs_0_.refs_2_.rest_0_), channel_id=1, source_target_pairs={{0,2},{1,3},{4,5},{5,4},{8,10},{9,11},{12,13},{13,12},{16,18},{17,... | collective-permute-start | bytes 786440 | tf_op jit(solution)/shard_map/ppermute | solution.py:319
  13.3 11.1 %collective-permute-start.5 = (bf16[8,32,512]{2,1,0:T(8,128)(2,1)S(1)}, bf16[8,32,512]{2,1,0:T(8,128)(2,1)S(1)}, u32[]{:S(2)}, u32[]{:S(2)}) collective-permute-start(bf16[8,32,512]{2,1,0:T(8,128)(2,1)S(1)} %mix.3), channel_id=1, source_target_pairs={{0,1},{2,3},{3,2},{4,6},{5,7},{8,9},{10,11},{11,10},{12,14},{13,15... | collective-permute-start | bytes 786440 | tf_op jit(solution)/shard_map/ppermute | solution.py:319
  15.8 8.6 %collective-permute-start.3 = (bf16[8,32,512]{2,1,0:T(8,128)(2,1)S(1)}, bf16[8,32,512]{2,1,0:T(8,128)(2,1)S(1)}, u32[]{:S(2)}, u32[]{:S(2)}) collective-permute-start(bf16[8,32,512]{2,1,0:T(8,128)(2,1)S(1)} %cross.1._.refs_0_.refs_2_.rest_0_), channel_id=1, source_target_pairs={{6,7},{14,15},{22,23},{30,31}} | collective-permute-start | bytes 786440 | tf_op jit(solution)/shard_map/ppermute | solution.py:319
  16.7 10.5 %collective-permute-start.2 = (bf16[8,32,512]{2,1,0:T(8,128)(2,1)S(1)}, bf16[8,32,512]{2,1,0:T(8,128)(2,1)S(1)}, u32[]{:S(2)}, u32[]{:S(2)}) collective-permute-start(bf16[8,32,512]{2,1,0:T(8,128)(2,1)S(1)} %mix.2), channel_id=1, source_target_pairs={{0,1},{2,3},{3,2},{4,6},{5,7},{8,9},{10,11},{11,10},{12,14},{13,15... | collective-permute-start | bytes 786440 | tf_op jit(solution)/shard_map/ppermute | solution.py:319
